TPU v7x, 256 devices: a whole 4x4x8 slice. The times are simulated.
256 devices in a mesh: dp: 32 (over x_lo, z, core), tp: 8 (over y, x_hi).
Axes of the slice: x: 4 (x_hi: 2, x_lo: 2; x = x_hi * 2 + x_lo), y: 4, z: 8, core: 2. Of those that a mesh axis runs over, the one named last changes fastest.
Arguments:
- gate_param: bfloat16 [4096, 14336], P(('dp', 'tp')), may hold values from -4 to 4
- up_param: bfloat16 [4096, 14336], P(('dp', 'tp')), may hold values from -4 to 4
- gate_grad: bfloat16 [4096, 14336], P(('dp', 'tp')), may hold values from -6 to 6
- up_grad: bfloat16 [4096, 14336], P(('dp', 'tp')), may hold values from -6 to 6
- gate_mom: bfloat16 [4096, 14336], P(('dp', 'tp')), may hold values from -2 to 2
- up_mom: bfloat16 [4096, 14336], P(('dp', 'tp')), may hold values from -2 to 2
- gate_var: bfloat16 [4096, 14336], P(('dp', 'tp')), may hold values from 0.049804688 to 1
- up_var: bfloat16 [4096, 14336], P(('dp', 'tp')), may hold values from 0.049804688 to 1
- queries: bfloat16 [1024, 2, 4096], P('dp', None, 'tp'), may hold values from -20 to 20
- new_keys: bfloat16 [1024, 2, 1024], P('dp', None, 'tp'), may hold values from -6 to 6
- new_values: bfloat16 [1024, 2, 1024], P('dp', None, 'tp'), may hold values from -6 to 6
- cache_keys: bfloat16 [1024, 192, 1024], P('dp', None, 'tp'), may hold values from -6 to 6
- cache_values: bfloat16 [1024, 192, 1024], P('dp', None, 'tp'), may hold values from -6 to 6
- cache_len: int32 [1024], P('dp'), may hold values from 2 to 192, as said below
- residual: bfloat16 [1024, 2, 4096], P('dp', None, 'tp'), may hold values from -180 to 180
- out_proj: bfloat16 [4096, 4096], P('tp'), may hold values from -0.09375 to 0.09375
- norm_gain: bfloat16 [4096], replicated, may hold values from 0.099609375 to 1.8984375
Outputs:
- gate_updated: bfloat16 [4096, 14336], P(('dp', 'tp'))
- up_updated: bfloat16 [4096, 14336], P(('dp', 'tp'))
- mixed_stream: bfloat16 [1024, 2, 4096], P('dp', None, 'tp')
- hidden: bfloat16 [1024, 2, 14336], P('dp', None, 'tp')
Inputs may be any that keep to these rules, and one draw needn't show every extreme that they name: `cache_len`: each group of 32 rows has a row with exactly 192 filled slots.
All inputs are finite; a program needn't handle non-finite values.
Results may differ from a plain program's by a relative error of at most 0.0082.
Values may be sent and summed in bfloat16 or wider, within the bound.
A program may use at most 128 MiB of HBM per device.

v0:
```python
import math

import jax
import jax.numpy as jnp
from jax import lax
from jax.sharding import PartitionSpec as P

HD = 128


beta_one = 0.9
beta_two = 0.95
adam_step = 20
learn_rate = 0.1
decay_rate = 0.1
epsilon_adam = 1e-08
epsilon_norm = 1e-05
masked_score = -1e30


def adamw_update(param, grad, moment, second):
    grad32 = grad.astype(jnp.float32)
    moment_new = beta_one * moment.astype(jnp.float32) + (1.0 - beta_one) * grad32
    second_new = beta_two * second.astype(jnp.float32) + (1.0 - beta_two) * grad32 * grad32
    corr_one = 1.0 - beta_one**adam_step
    corr_two = 1.0 - beta_two**adam_step
    direction = moment_new / corr_one / (jnp.sqrt(second_new / corr_two) + epsilon_adam)
    param32 = param.astype(jnp.float32)
    return (param32 - learn_rate * (direction + decay_rate * param32)).astype(jnp.bfloat16)


def attention(queries, new_keys, new_values, cache_keys, cache_values, cache_len):
    batch_rows = queries.shape[0]
    query_width = queries.shape[2]
    kv_heads = new_keys.shape[2] // HD
    groups = query_width // HD // kv_heads
    slots = cache_keys.shape[1]
    query_heads = queries.reshape(batch_rows, 2, kv_heads, groups, HD)
    keys_cache = cache_keys.reshape(batch_rows, slots, kv_heads, HD)
    vals_cache = cache_values.reshape(batch_rows, slots, kv_heads, HD)
    keys_fresh = new_keys.reshape(batch_rows, 2, kv_heads, HD)
    vals_fresh = new_values.reshape(batch_rows, 2, kv_heads, HD)
    scale = 1.0 / math.sqrt(HD)
    score_cache = (
        jnp.einsum("rskgd,rtkd->rskgt", query_heads, keys_cache, preferred_element_type=jnp.float32)
        * scale
    )
    score_fresh = (
        jnp.einsum("rskgd,rukd->rskgu", query_heads, keys_fresh, preferred_element_type=jnp.float32)
        * scale
    )
    valid_cache = jnp.arange(slots, dtype=jnp.int32)[None, :] < cache_len[:, None]
    valid_fresh = jnp.arange(2, dtype=jnp.int32)[None, :] <= jnp.arange(2, dtype=jnp.int32)[:, None]
    score_cache = jnp.where(valid_cache[:, None, None, None, :], score_cache, masked_score)
    score_fresh = jnp.where(valid_fresh[None, :, None, None, :], score_fresh, masked_score)
    scores = jnp.concatenate([score_cache, score_fresh], axis=-1)
    top = jnp.max(scores, axis=-1, keepdims=True)
    expo = jnp.exp(scores - top)
    weights = (expo / jnp.sum(expo, axis=-1, keepdims=True)).astype(jnp.bfloat16)
    context = jnp.einsum(
        "rskgt,rtkd->rskgd", weights[..., :slots], vals_cache, preferred_element_type=jnp.float32
    )
    context = context + jnp.einsum(
        "rskgu,rukd->rskgd", weights[..., slots:], vals_fresh, preferred_element_type=jnp.float32
    )
    return context.reshape(batch_rows, 2, query_width).astype(jnp.bfloat16)


def rms_norm(mixed, gain):
    mixed32 = mixed.astype(jnp.float32)
    factor = lax.rsqrt(jnp.mean(mixed32 * mixed32, axis=-1, keepdims=True) + epsilon_norm)
    return (mixed32 * factor * gain.astype(jnp.float32)).astype(jnp.bfloat16)


def on_device(
    gate_param,
    up_param,
    gate_grad,
    up_grad,
    gate_mom,
    up_mom,
    gate_var,
    up_var,
    queries,
    new_keys,
    new_values,
    cache_keys,
    cache_values,
    cache_len,
    residual,
    out_proj,
    norm_gain,
):
    gate_updated = adamw_update(gate_param, gate_grad, gate_mom, gate_var)
    up_updated = adamw_update(up_param, up_grad, up_mom, up_var)
    stacked = jnp.stack([gate_updated, up_updated], axis=1)
    regrouped = lax.all_to_all(stacked, "tp", split_axis=2, concat_axis=0, tiled=True)
    block_rows = regrouped.shape[0]
    hidden_cols = regrouped.shape[2]
    blocks = regrouped.reshape(block_rows, 2 * hidden_cols)
    context = attention(queries, new_keys, new_values, cache_keys, cache_values, cache_len)
    batch_rows = context.shape[0]
    token_rows = batch_rows * 2
    flat = context.reshape(token_rows, context.shape[2])
    local_width = residual.shape[2]
    model_width = local_width * lax.axis_size("tp")
    stream = residual.reshape(token_rows, local_width)
    tp_index = lax.axis_index("tp")
    total = lax.psum(jnp.dot(flat, out_proj, preferred_element_type=jnp.float32), "tp")
    stream_all = lax.all_gather(stream, "tp", axis=1, tiled=True)
    mixed_all = (stream_all.astype(jnp.float32) + total).astype(jnp.bfloat16)
    normed = rms_norm(mixed_all, norm_gain)
    mixed_local = lax.dynamic_slice_in_dim(mixed_all, tp_index * local_width, local_width, 1)
    activations = jnp.dot(
        normed, lax.all_gather(blocks, "dp", axis=0, tiled=True), preferred_element_type=jnp.float32
    )
    scale_in = 1.0 / math.sqrt(model_width)
    gate_act = activations[:, :hidden_cols] * scale_in
    up_act = activations[:, hidden_cols:] * scale_in
    hidden = (jax.nn.silu(gate_act) * up_act).astype(jnp.bfloat16)
    return (
        gate_updated,
        up_updated,
        mixed_local.reshape(batch_rows, 2, local_width),
        hidden.reshape(batch_rows, 2, hidden_cols),
    )


def solution(mesh):
    placed = (
        P(("dp", "tp"), None),
        P(("dp", "tp"), None),
        P(("dp", "tp"), None),
        P(("dp", "tp"), None),
        P(("dp", "tp"), None),
        P(("dp", "tp"), None),
        P(("dp", "tp"), None),
        P(("dp", "tp"), None),
        P("dp", None, "tp"),
        P("dp", None, "tp"),
        P("dp", None, "tp"),
        P("dp", None, "tp"),
        P("dp", None, "tp"),
        P("dp"),
        P("dp", None, "tp"),
        P("tp", None),
        P(),
    )
    return jax.shard_map(
        on_device,
        mesh=mesh,
        in_specs=placed,
        out_specs=(
            P(("dp", "tp"), None),
            P(("dp", "tp"), None),
            P("dp", None, "tp"),
            P("dp", None, "tp"),
        ),
        check_vma=False,
    )
```

profile of v0, /device:TPU:1, one launch (start us, length us, event | category | flops | bytes accessed | tf_op | source)
XLA Modules:
  0.0 291.3 jit_solution(14697434603929935690)
XLA Ops:
  8.0 0.0 copy-start
  8.0 0.0 all-reduce.2.cloned.1.call-start
  8.1 1.0 reshape.178
  9.1 0.0 copy-start.1
  9.1 0.9 iota_compare_fusion
  10.0 0.0 copy-done
  10.0 1.0 fusion.61
  11.0 1.0 fusion.62
  12.0 0.4 fusion.58
  12.4 0.3 divide_convert_fusion
  12.7 0.0 copy-start.4
  12.7 0.0 copy-start.5
  12.8 0.0 copy-start.6
  12.8 0.0 copy-start.7
  12.8 1.1 fusion.57
  13.9 1.9 fusion.14
  15.8 0.0 copy-done.1
  15.8 1.8 fusion.54
  17.6 0.0 all-reduce.2.cloned.1.call-update
  17.7 0.0 all-gather.2.cloned.1.call-start
  17.7 0.0 copy-done.4
  17.7 0.0 copy-done.5
  17.7 0.0 copy-done.6
  17.7 0.0 copy-done.7
  17.7 3.1 %fusion.29 = (bf16[16,14336]{1,0:T(8,128)(2,1)S(1)}, bf16[16,14336]{1,0:T(8,128)(2,1)S(1)}) fusion(bf16[16,14336]{1,0:T(8,128)(2,1)S(1)} %copy-done.4, bf16[16,14336]{1,0:T(8,128)(2,1)S(1)} %copy-done.5, bf16[16,14336]{1,0:T(8,128)(2,1)S(1)} %copy-done.6, bf16[16,14336]{1,0:T(8,128)(2,1)S(1)} %copy-done.7, bf16[16,14336]{1,0:T(8,128)(2,1)} %param.24, ...), kind=kLoop, calls=%fused_computation.29 | loop fusion | flops 9175040 | bytes 4587520 | tf_op jit(solution)/shard_map/convert_element_type | solution.py:29
  20.8 0.0 copy-start.2
  20.8 0.0 copy-start.3
  20.8 0.7 copy-done.2
  21.6 0.1 copy-done.3
  21.7 0.1 pad_maximum_fusion
  21.8 11.4 %copy.46 = bf16[16,2,14336]{0,1,2:T(2,128)(2,1)} copy(bf16[16,2,14336]{2,0,1:T(8,128)(2,1)S(1)} %pad_maximum_fusion) | data formatting | bytes 1835008 | tf_op jit(solution)/shard_map/stack | solution.py:96
  33.3 9.6 %reshape.188 = bf16[8,2,28672]{2,1,0:T(2,128)(2,1)S(1)} reshape(bf16[14336,2,16]{2,1,0:T(2,128)(2,1)} %bitcast.80) | data formatting | bytes 1835008
  42.8 29.1 %all_to_all.15 = bf16[8,2,28672]{2,1,0:T(2,128)(2,1)S(1)} all-to-all(bf16[8,2,28672]{2,1,0:T(2,128)(2,1)S(1)} %reshape.188), channel_id=1, replica_groups=mesh['dp'=32,'tp'=8] {'tp'}, dimensions={0} | all-to-all | bytes 1835008 | tf_op jit(solution)/shard_map/all_to_all | solution.py:97
  72.0 7.0 %reshape.189 = bf16[14336,2,16]{2,1,0:T(2,128)(2,1)} reshape(bf16[8,2,28672]{2,1,0:T(2,128)(2,1)S(1)} %all_to_all.15) | data formatting | bytes 1835008
  79.0 0.0 copy-start.8
  79.0 0.0 copy-start.9
  79.0 15.1 %copy.47 = bf16[16,2,8,1792]{3,1,0,2:T(2,128)(2,1)S(1)} copy(bf16[16,2,8,1792]{0,1,3,2:T(2,128)(2,1)} %bitcast.81) | data formatting | bytes 1835008 | tf_op jit(solution)/shard_map/all_to_all | solution.py:97
  94.1 1.0 copy.55
  95.1 0.0 all-gather.2.cloned.1.call-update
  95.1 0.0 copy-done.8
  95.2 0.0 copy-done.9
  95.2 33.5 %all_gather.6 = bf16[64,4096]{1,0:T(8,128)(2,1)S(1)} all-gather(bf16[64,512]{1,0:T(8,128)(2,1)S(1)} %reshape.177), channel_id=1, replica_groups=mesh['dp'=32,'tp'=8] {'tp'}, dimensions={1}, use_global_device_ids=true | all-gather | bytes 589824 | tf_op jit(solution)/shard_map/all_gather | solution.py:110
  128.7 15.7 %all-reduce.2.cloned.1.call-done = f32[64,4096]{1,0:T(8,128)} async-done(((f32[64,4096]{1,0:T(8,128)}), f32[64,4096]{1,0:T(8,128)}) %all-reduce.2.cloned.1.call-update) | async-done | bytes 1048592 | tf_op jit(solution)/shard_map/psum | solution.py:109
  144.5 1.5 fusion.24
  146.0 0.7 reshape.181
  146.6 124.2 %all-gather.2.cloned.1.call-done = bf16[4096,3584]{1,0:T(8,128)(2,1)} async-done(((bf16[128,3584]{1,0:T(8,128)(2,1)}), bf16[4096,3584]{1,0:T(8,128)(2,1)}) %all-gather.2.cloned.1.call-update) | async-done | bytes 29360144 | tf_op jit(solution)/shard_map/all_gather | solution.py:115
  270.8 12.1 %fusion.47 = f32[64,3584]{1,0:T(8,128)S(1)} fusion(bf16[4096,3584]{1,0:T(8,128)(2,1)} %all-gather.2.cloned.1.call-done, bf16[64,4096]{1,0:T(8,128)(2,1)S(1)} %get-tuple-element.9, f32[4096]{0:T(1024)S(1)} %convert_element_type.94, f32[64]{0:T(128)S(1)} %add_rsqrt_fusion), kind=kOutput, calls=%fused_computation.48 | convolution fusion | flops 1880096768 | bytes 30818560 | tf_op jit(solution)/shard_map/dot_general | solution.py:114
  282.9 0.2 fusion.52
  283.1 0.8 reshape.183
  (6 shorter events, 0.1 us)
Async XLA Ops:
  8.0 2.0 copy-start
  8.0 136.4 %all-reduce.2.cloned.1.call-start = ((), (), s32[]{:S(2)}) async-start(), calls=%async_computation.1 | async-start | bytes 2097152 | tf_op jit(solution)/shard_map/psum | solution.py:109
  9.1 6.7 %copy-start.1 = (bf16[512,4096]{1,0:T(8,128)(2,1)S(1)}, bf16[512,4096]{1,0:T(8,128)(2,1)}, u32[]{:S(2)}) copy-start(bf16[512,4096]{1,0:T(8,128)(2,1)} %param.32) | copy-start | bytes 12582916
  12.7 5.0 %copy-start.4 = (bf16[16,14336]{1,0:T(8,128)(2,1)S(1)}, bf16[16,14336]{1,0:T(8,128)(2,1)}, u32[]{:S(2)}) copy-start(bf16[16,14336]{1,0:T(8,128)(2,1)} %param.17) | copy-start | bytes 1376260
  12.7 5.0 %copy-start.5 = (bf16[16,14336]{1,0:T(8,128)(2,1)S(1)}, bf16[16,14336]{1,0:T(8,128)(2,1)}, u32[]{:S(2)}) copy-start(bf16[16,14336]{1,0:T(8,128)(2,1)} %param.19) | copy-start | bytes 1376260
  12.8 5.0 %copy-start.6 = (bf16[16,14336]{1,0:T(8,128)(2,1)S(1)}, bf16[16,14336]{1,0:T(8,128)(2,1)}, u32[]{:S(2)}) copy-start(bf16[16,14336]{1,0:T(8,128)(2,1)} %param.23) | copy-start | bytes 1376260
  12.8 5.0 %copy-start.7 = (bf16[16,14336]{1,0:T(8,128)(2,1)S(1)}, bf16[16,14336]{1,0:T(8,128)(2,1)}, u32[]{:S(2)}) copy-start(bf16[16,14336]{1,0:T(8,128)(2,1)} %param.21) | copy-start | bytes 1376260
  17.7 253.2 %all-gather.2.cloned.1.call-start = ((), (), s32[]{:S(2)}) async-start(), calls=%async_computation.2 | async-start | bytes 30277632 | tf_op jit(solution)/shard_map/all_gather | solution.py:115
  20.8 0.8 copy-start.2
  20.8 0.9 copy-start.3
  79.0 16.2 %copy-start.8 = (bf16[32,2,512]{2,1,0:T(2,128)(2,1)S(1)}, bf16[32,2,512]{2,1,0:T(2,128)(2,1)}, u32[]{:S(2)}) copy-start(bf16[32,2,512]{2,1,0:T(2,128)(2,1)} %param.31) | copy-start | bytes 196612
  79.0 16.2 %copy-start.9 = (bf16[4096]{0:T(1024)(128)(2,1)S(1)}, bf16[4096]{0:T(1024)(128)(2,1)}, u32[]{:S(2)}) copy-start(bf16[4096]{0:T(1024)(128)(2,1)} %param.33) | copy-start | bytes 24580
Sparse Core Ops, SparseCore 0:
  17.8 126.6 all-reduce.1
Sparse Core Ops, SparseCore 1:
  95.2 175.6 all-gather.1
where the time goes:
time: 292 us; the launch traced here: 291 us
  waiting for transfers between devices  140 us (48%)
  blocking collectives  62.6 us (21%)
  local copies, waits for them, and re-layouts  47.6 us (16%)
  matrix products  19 us (7%)
  between operations  15.7 us (5%)
  other arithmetic  6.37 us (2%)
    all_gather x1, waiting for transfers between devices, on_device(): lax.all_gather(blocks, 'dp', axis=0, tiled=True)  124 us
    all_gather x1, blocking collectives, on_device(): stream_all = lax.all_gather(stream, 'tp', axis=1, tiled=True)  33.5 us
    all_to_all x1, blocking collectives, on_device(): lax.all_to_all(stacked, 'tp', split_axis=2, concat_axis=0, tiled=True)  29.1 us
    unnamed x23, local copies, waits for them, and re-layouts  18.6 us
    psum x1, waiting for transfers between devices, on_device(): lax.psum(jnp.dot(flat, out_proj, preferred_element_type=jnp.float32), 'tp')  15.7 us
    all_to_all x1, local copies, waits for them, and re-layouts, on_device(): lax.all_to_all(stacked, 'tp', split_axis=2, concat_axis=0, tiled=True)  15.1 us
    dot_general x1, matrix products, on_device(): jnp.dot(normed, lax.all_gather(blocks, 'dp', axis=0, tiled=True), preferr...  12.1 us
    another operation x1, local copies, waits for them, and re-layouts, on_device(): stacked = jnp.stack([gate_updated, up_updated], axis=1)  11.4 us
  transfers between devices with their start and end apart: 2, of which 2 were waited for; matrix products, arithmetic and copies ran while one was open for 17% of the time, Pallas kernels for 0%

commit v1 on v0

v1 whole, which is shorter than its diff:
```python
import functools
import math

import jax
import jax.numpy as jnp
from jax import lax
from jax.experimental import pallas as pl
from jax.experimental.pallas import tpu as pltpu
from jax.sharding import PartitionSpec as P

MESH = pl.DeviceIdType.MESH
F32 = jnp.float32
BF16 = jnp.bfloat16

HD = 128
ROWS = 32
SLOTS = 192
PADDED = 208
D = 4096
FF = 14336
NZ, NY = 8, 4
PLANE = NZ * NY
WIDTHS = (512, 384)
PAIR = 896

beta_one = 0.9
beta_two = 0.95
adam_step = 20
learn_rate = 0.1
decay_rate = 0.1
epsilon_adam = 1e-08
epsilon_norm = 1e-05
masked_score = -1e30


def adamw_update(param, grad, moment, second):
    grad32 = grad.astype(F32)
    moment_new = beta_one * moment.astype(F32) + (1.0 - beta_one) * grad32
    second_new = beta_two * second.astype(F32) + (1.0 - beta_two) * grad32 * grad32
    corr_one = 1.0 - beta_one**adam_step
    corr_two = 1.0 - beta_two**adam_step
    direction = moment_new * (1.0 / corr_one) / (
        jnp.sqrt(second_new * (1.0 / corr_two)) + epsilon_adam
    )
    param32 = param.astype(F32)
    return param32 - learn_rate * (direction + decay_rate * param32)


def kernel(
    gp, up, gg, ug, gm, um, gv, uv,
    q_in, nk_in, nv_in, ck_in, cv_in, len_in, res_in, wo_in, gain_in,
    g_out, u_out, mix_out, hid_out,
    adam, gnew, unew, sbuf0, sbuf1, wbuf0, wbuf1,
    qbuf, kbuf, vbuf, lens, res, wo, gain,
    ctx32, ctxb, pbuf, rsbuf, rres, ybuf, mixb, abuf, hbuf, obuf, hfin,
    load_sem, send_sem, a2a_sem, x1_sem, x2_sem, core_sem,
    rs_sem, res_sem, y_sem, zr_sem, mix_sem, out_sem, store_sem,
):
    dp = lax.axis_index("dp")
    tp = lax.axis_index("tp")
    x_lo = dp // 16
    z = (dp // 2) % NZ
    c = dp % 2
    y = tp // 2
    h = tp % 2
    x = h * 2 + x_lo
    other = 1 - h

    def place(xx, yy, zz, cc):
        return ((xx % 2) * 16 + zz * 2 + cc, yy * 2 + xx // 2)

    right = (x + 1) % 4
    left = (x + 3) % 4
    across = (x + 2) % 4
    z_up = (z + 1) % NZ
    z_dn = (z + NZ - 1) % NZ

    loads = []
    for i, ref in enumerate((gp, gg, gm, gv, up, ug, um, uv)):
        loads.append(pltpu.make_async_copy(ref, adam.at[i], load_sem.at[i]))
    load_q = pltpu.make_async_copy(q_in, qbuf, load_sem.at[8])
    load_k = pltpu.make_async_copy(ck_in, kbuf.at[:, pl.ds(0, SLOTS), :], load_sem.at[9])
    load_nk = pltpu.make_async_copy(nk_in, kbuf.at[:, pl.ds(SLOTS, 16), :], load_sem.at[10])
    load_v = pltpu.make_async_copy(cv_in, vbuf.at[:, pl.ds(0, SLOTS), :], load_sem.at[11])
    load_nv = pltpu.make_async_copy(nv_in, vbuf.at[:, pl.ds(SLOTS, 16), :], load_sem.at[12])
    load_len = pltpu.make_async_copy(len_in, lens, load_sem.at[13])
    load_res = pltpu.make_async_copy(res_in, res, load_sem.at[14])
    load_wo = pltpu.make_async_copy(wo_in, wo, load_sem.at[15])
    load_gain = pltpu.make_async_copy(gain_in, gain, load_sem.at[16])
    for copy in loads:
        copy.start()
    for copy in (load_res, load_q, load_k, load_nk, load_len, load_v, load_nv, load_wo, load_gain):
        copy.start()

    barrier = pltpu.get_barrier_semaphore()

    def greet(where):
        pl.semaphore_signal(barrier, inc=1, device_id=where, device_id_type=MESH)

    @pl.loop(1, PLANE)
    def _(o):
        greet(place(x, (y + o // NZ) % NY, (z + o % NZ) % NZ, c))

    @pl.loop(1, NZ)
    def _(o):
        greet(place(across, y, (z + o) % NZ, c))

    @pl.loop(0, NY)
    def _(o):
        greet(place(across, (y + o) % NY, z, c))

    greet(place(right, y, z, c))
    greet(place(left, y, z, c))
    greet(place(x, y, z, 1 - c))

    for copy in loads:
        copy.wait()
    lane16 = lax.broadcasted_iota(jnp.int32, (16, 128), 1)

    @pl.loop(0, 16)
    def _(pair):
        cols = pl.ds(pl.multiple_of(pair * PAIR, 128), PAIR)
        new = []
        for first, dest in ((0, gnew), (4, unew)):
            value = adamw_update(
                adam[first, :, cols],
                adam[first + 1, :, cols],
                adam[first + 2, :, cols],
                adam[first + 3, :, cols],
            )
            dest[:, cols] = value.astype(BF16)
            new.append(value)
        gate = [new[0][:, i * 128 : (i + 1) * 128] for i in range(7)]
        upper = [new[1][:, i * 128 : (i + 1) * 128] for i in range(7)]
        turned = pltpu.roll(upper[3], 64, 1)
        mixed_even = jnp.where(lane16 < 64, gate[3], turned)
        mixed_odd = jnp.where(lane16 < 64, turned, gate[3])
        for half, (a, b, d, middle) in enumerate(((0, 1, 2, mixed_even), (4, 5, 6, mixed_odd))):
            for i, tile in enumerate((gate[a], upper[a], gate[b], upper[b])):
                sbuf0[2 * pair + half, :, i * 128 : (i + 1) * 128] = tile.astype(BF16)
            for i, tile in enumerate((gate[d], upper[d], middle)):
                sbuf1[2 * pair + half, :, i * 128 : (i + 1) * 128] = tile.astype(BF16)

    store_g = pltpu.make_async_copy(gnew, g_out, store_sem.at[0])
    store_u = pltpu.make_async_copy(unew, u_out, store_sem.at[1])
    store_g.start()
    store_u.start()

    pl.semaphore_wait(barrier, PLANE - 1 + NZ - 1 + NY + 3)

    sbufs = (sbuf0, sbuf1)
    wbufs = (wbuf0, wbuf1)

    def remote(src, dst, send, recv, where):
        return pltpu.make_async_remote_copy(
            src_ref=src,
            dst_ref=dst,
            send_sem=send,
            recv_sem=recv,
            device_id=where,
            device_id_type=MESH,
        )

    for q in range(2):
        @pl.loop(1, PLANE)
        def _(o, q=q):
            yy = (y + o // NZ) % NY
            zz = (z + o % NZ) % NZ
            remote(
                sbufs[q].at[yy * NZ + zz],
                wbufs[q].at[x_lo, z, c, y, h],
                send_sem.at[q],
                a2a_sem.at[q],
                place(x, yy, zz, c),
            ).start()

        wbufs[q][x_lo, z, c, y, h] = sbufs[q][y * NZ + z]

    load_res.wait()
    to_across = place(across, y, z, c)
    res_copy = remote(res.at[other], rres.at[h], send_sem.at[2], res_sem, to_across)
    res_copy.start()
    rres[h] = res[h]

    for copy in (load_q, load_k, load_nk, load_len, load_v, load_nv):
        copy.wait()
    part = 8

    @pl.loop(0, ROWS // part)
    def _(i):
        rows = pl.ds(pl.multiple_of(i * part, part), part)
        slot = lax.broadcasted_iota(jnp.int32, (part, 8, PADDED), 2)
        token = lax.broadcasted_iota(jnp.int32, (part, 8, PADDED), 1) // 4
        scores = lax.dot_general(
            qbuf[rows], kbuf[rows], (((2,), (2,)), ((0,), (0,))), preferred_element_type=F32
        ) * (1.0 / math.sqrt(HD))
        filled = lens[rows][:, :, 0:1]
        fresh = (slot >= SLOTS) & (slot <= SLOTS + token)
        scores = jnp.where((slot < filled) | fresh, scores, masked_score)
        expo = jnp.exp(scores - jnp.max(scores, axis=-1, keepdims=True))
        weights = (expo / jnp.sum(expo, axis=-1, keepdims=True)).astype(BF16)
        context = lax.dot_general(
            weights, vbuf[rows], (((2,), (1,)), ((0,), (0,))), preferred_element_type=F32
        )
        ctx32[rows] = context

    for s in range(2):
        for g in range(4):
            ctxb[s * ROWS : (s + 1) * ROWS, g * HD : (g + 1) * HD] = ctx32[:, s * 4 + g, :].astype(BF16)

    def held(q, xx):
        return wbufs[q].at[xx % 2, :, c, :, xx // 2]

    def held_half(q, xx, half):
        return wbufs[q].at[xx % 2, pl.ds(half * 4, 4), c, :, xx // 2]

    def wait_a2a(q):
        some = sbufs[q].at[pl.ds(0, PLANE - 1)]
        remote(some, some, send_sem.at[q], a2a_sem.at[q], to_across).wait_recv()

    to_right = place(right, y, z, c)
    to_left = place(left, y, z, c)
    to_twin = place(x, y, z, 1 - c)

    def stage_one(q):
        mine = held(q, x)
        for side, where in enumerate((to_right, to_left)):
            remote(mine, mine, send_sem.at[3 + q], x1_sem.at[2 * q + side], where).start()
        remote(mine, mine, send_sem.at[7 + q], core_sem.at[q], to_twin).start()

    def stage_two(q):
        from_left, from_right = held(q, left), held(q, right)
        remote(from_left, from_left, send_sem.at[3 + q], x1_sem.at[2 * q], to_right).wait_recv()
        half = held_half(q, left, 0)
        remote(half, half, send_sem.at[5 + q], x2_sem.at[2 * q], to_right).start()
        remote(from_right, from_right, send_sem.at[3 + q], x1_sem.at[2 * q + 1], to_left).wait_recv()
        half = held_half(q, right, 1)
        remote(half, half, send_sem.at[5 + q], x2_sem.at[2 * q + 1], to_left).start()
        for part in (from_left, from_right):
            remote(part, part, send_sem.at[7 + q], core_sem.at[q], to_twin).start()

    def stage_three(q):
        for side in range(2):
            half = held_half(q, across, side)
            remote(half, half, send_sem.at[5 + q], x2_sem.at[2 * q + side], to_right).wait_recv()
        part = held(q, across)
        remote(part, part, send_sem.at[7 + q], core_sem.at[q], to_twin).start()

    wait_a2a(0)
    stage_one(0)

    load_wo.wait()

    @pl.loop(0, 8)
    def _(j):
        cols = pl.ds(pl.multiple_of(j * 512, 512), 512)
        partial = jnp.dot(ctxb[...], wo[:, cols], preferred_element_type=F32).astype(BF16)
        pbuf[j, 0] = partial[:ROWS]
        pbuf[j, 1] = partial[ROWS:]

    @pl.loop(1, 8)
    def _(o):
        yy = (y + o // 2) % NY
        hh = (h + o) % 2
        remote(
            pbuf.at[pl.ds(2 * yy, 2), hh],
            rsbuf.at[tp],
            send_sem.at[9],
            rs_sem,
            place(hh * 2 + x_lo, yy, z, c),
        ).start()

    rsbuf[tp] = pbuf[pl.ds(2 * y, 2), h]
    wait_a2a(1)
    stage_one(1)
    stage_two(0)

    some = rsbuf.at[pl.ds(0, 7)]
    remote(some, some, send_sem.at[9], rs_sem, to_across).wait_recv()
    remote(res.at[0], rres.at[0], send_sem.at[2], res_sem, to_across).wait_recv()
    for k in range(2):
        total = rsbuf[0, k].astype(F32)
        for i in range(1, 8):
            total = total + rsbuf[i, k].astype(F32)
        ybuf[2 * y + k] = (rres[k].astype(F32) + total).astype(BF16)

    mine = ybuf.at[pl.ds(2 * y, 2)]
    for o in range(1, NY):
        remote(mine, mine, send_sem.at[10], y_sem, place(x, (y + o) % NY, z, c)).start()
    remote(ybuf.at[2 * y + other], mixb.at[h], send_sem.at[11], mix_sem, to_across).start()
    mixb[h] = ybuf[2 * y + h]
    some = ybuf.at[pl.ds(0, 6)]
    remote(some, some, send_sem.at[10], y_sem, to_across).wait_recv()
    load_gain.wait()
    square = jnp.zeros((ROWS, 1), F32)
    for j in range(8):
        value = ybuf[j].astype(F32)
        square = square + jnp.sum(value * value, axis=-1, keepdims=True)
    factor = lax.rsqrt(square * (1.0 / D) + epsilon_norm)
    for j in range(8):
        cols = slice(j * 512, (j + 1) * 512)
        abuf[z, :, cols] = (
            ybuf[j].astype(F32) * factor * gain[:, cols].astype(F32)
        ).astype(BF16)

    to_up = place(x, y, z_up, c)
    to_dn = place(x, y, z_dn, c)

    def ring(step, up_ref, dn_ref):
        remote(up_ref, up_ref, send_sem.at[12], zr_sem.at[2 * step], to_up).start()
        remote(dn_ref, dn_ref, send_sem.at[12], zr_sem.at[2 * step + 1], to_dn).start()

    def ring_wait(step, up_ref, dn_ref):
        remote(up_ref, up_ref, send_sem.at[12], zr_sem.at[2 * step], to_up).wait_recv()
        remote(dn_ref, dn_ref, send_sem.at[12], zr_sem.at[2 * step + 1], to_dn).wait_recv()

    def block(shift):
        return abuf.at[(z + NZ + shift) % NZ]

    ring(0, block(0), block(0))
    stage_two(1)
    ring_wait(0, block(-1), block(1))
    ring(1, block(-1), block(1))
    stage_three(0)
    ring_wait(1, block(-2), block(2))
    ring(2, block(-2), block(2))
    ring_wait(2, block(-3), block(3))
    low, high = pl.ds(0, 16), pl.ds(16, 16)
    ring(3, block(-3).at[low], block(3).at[high])
    stage_three(1)
    ring_wait(3, block(4).at[low], block(4).at[high])

    def core_wait(q):
        both = wbufs[q].at[:, :, 1 - c]
        remote(both, both, send_sem.at[7 + q], core_sem.at[q], to_twin).wait_recv()

    scale = 1.0 / math.sqrt(D)

    def product(q):
        acts = jnp.zeros((NZ * ROWS, WIDTHS[q]), F32)
        for k in range(4):
            left_side = abuf[:, :, k * 1024 : (k + 1) * 1024].reshape(NZ * ROWS, 1024)
            right_side = wbufs[q][k // 2, (k % 2) * 4 : (k % 2) * 4 + 4].reshape(1024, WIDTHS[q])
            acts = acts + jnp.dot(left_side, right_side, preferred_element_type=F32)
        return acts * scale

    def gated(gate, upper):
        value = gate / (1.0 + jnp.exp(-gate)) * upper
        return value.astype(BF16).reshape(NZ, ROWS, 128)

    core_wait(0)
    acts = product(0)
    hbuf[:, :, 0:128] = gated(acts[:, 0:128], acts[:, 128:256])
    hbuf[:, :, 128:256] = gated(acts[:, 256:384], acts[:, 384:512])
    core_wait(1)
    acts = product(1)
    hbuf[:, :, 256:384] = gated(acts[:, 0:128], acts[:, 128:256])
    hbuf[:, :, 384:512] = gated(acts[:, 256:384], pltpu.roll(acts[:, 256:384], 64, 1))

    owner = (z // 4) * 2 + x_lo

    @pl.loop(1, NZ)
    def _(o):
        zz = (z + o) % NZ
        remote(
            hbuf.at[zz], obuf.at[h, z % 4], send_sem.at[13], out_sem, place(owner, y, zz, c)
        ).start()

    stays = z // 4 == h

    @pl.when(stays)
    def _():
        pltpu.make_async_copy(hbuf.at[z], obuf.at[h, z % 4], out_sem).start()

    @pl.when(jnp.logical_not(stays))
    def _():
        remote(
            hbuf.at[z], obuf.at[h, z % 4], send_sem.at[13], out_sem, place(across, y, z, c)
        ).start()

    remote(mixb.at[0], mixb.at[0], send_sem.at[11], mix_sem, to_across).wait_recv()
    store_mix = pltpu.make_async_copy(mixb, mix_out, store_sem.at[2])
    store_mix.start()

    remote(obuf, obuf, send_sem.at[13], out_sem, to_across).wait_recv()
    lane = lax.broadcasted_iota(jnp.int32, (2, ROWS, 128), 2)
    for p in range(2):
        even, odd = obuf[:, 2 * p], obuf[:, 2 * p + 1]
        base = p * PAIR
        hfin[:, :, base : base + 384] = even[:, :, 0:384]
        hfin[:, :, base + 384 : base + 512] = jnp.where(
            lane < 64, even[:, :, 384:512], odd[:, :, 384:512]
        )
        hfin[:, :, base + 512 : base + 896] = odd[:, :, 0:384]
    store_hid = pltpu.make_async_copy(hfin, hid_out, store_sem.at[3])
    store_hid.start()

    def sent(index, ref):
        remote(ref, ref, send_sem.at[index], mix_sem, to_across).wait_send()

    for q in range(2):
        sent(q, sbufs[q].at[pl.ds(0, PLANE - 1)])
        for _ in range(2):
            sent(3 + q, held(q, x))
        for _ in range(2):
            sent(5 + q, held_half(q, left, 0))
        sent(7 + q, wbufs[q].at[:, :, c])
    sent(2, res.at[0])
    sent(9, rsbuf.at[pl.ds(0, 7)])
    sent(10, ybuf.at[pl.ds(0, 6)])
    sent(11, ybuf.at[0])
    sent(12, abuf.at[pl.ds(0, 7)])
    sent(13, hbuf.at[pl.ds(0, 7)])

    @pl.when(jnp.logical_not(stays))
    def _():
        sent(13, hbuf.at[0])

    store_g.wait()
    store_u.wait()
    store_mix.wait()
    store_hid.wait()


def on_device(
    gate_param,
    up_param,
    gate_grad,
    up_grad,
    gate_mom,
    up_mom,
    gate_var,
    up_var,
    queries,
    new_keys,
    new_values,
    cache_keys,
    cache_values,
    cache_len,
    residual,
    out_proj,
    norm_gain,
):
    q_rows = queries.reshape(ROWS, 8, HD)
    pad = ((0, 0), (0, 14), (0, 0))
    keys_fresh = jnp.pad(new_keys, pad)
    vals_fresh = jnp.pad(new_values, pad)
    lens = jnp.broadcast_to(cache_len[:, None, None], (ROWS, 1, 128))
    res = residual.transpose(1, 0, 2)
    gain = norm_gain.reshape(1, D)
    dma = pltpu.SemaphoreType.DMA
    vmem = pltpu.VMEM
    anywhere = pl.BlockSpec(memory_space=pl.ANY)
    gate_updated, up_updated, mixed, hidden = pl.pallas_call(
        kernel,
        out_shape=(
            jax.ShapeDtypeStruct((16, FF), BF16),
            jax.ShapeDtypeStruct((16, FF), BF16),
            jax.ShapeDtypeStruct((2, ROWS, 512), BF16),
            jax.ShapeDtypeStruct((2, ROWS, 1792), BF16),
        ),
        in_specs=[anywhere] * 17,
        out_specs=[anywhere] * 4,
        scratch_shapes=[
            vmem((8, 16, FF), BF16),
            vmem((16, FF), BF16),
            vmem((16, FF), BF16),
            vmem((PLANE, 16, WIDTHS[0]), BF16),
            vmem((PLANE, 16, WIDTHS[1]), BF16),
            vmem((2, NZ, 2, NY, 2, 16, WIDTHS[0]), BF16),
            vmem((2, NZ, 2, NY, 2, 16, WIDTHS[1]), BF16),
            vmem((ROWS, 8, HD), BF16),
            vmem((ROWS, PADDED, HD), BF16),
            vmem((ROWS, PADDED, HD), BF16),
            vmem((ROWS, 1, 128), jnp.int32),
            vmem((2, ROWS, 512), BF16),
            vmem((512, D), BF16),
            vmem((1, D), BF16),
            vmem((ROWS, 8, HD), F32),
            vmem((2 * ROWS, 512), BF16),
            vmem((8, 2, ROWS, 512), BF16),
            vmem((8, 2, ROWS, 512), BF16),
            vmem((2, ROWS, 512), BF16),
            vmem((8, ROWS, 512), BF16),
            vmem((2, ROWS, 512), BF16),
            vmem((NZ, ROWS, D), BF16),
            vmem((NZ, ROWS, 512), BF16),
            vmem((2, 4, ROWS, 512), BF16),
            vmem((2, ROWS, 1792), BF16),
            dma((17,)),
            dma((14,)),
            dma((2,)),
            dma((4,)),
            dma((4,)),
            dma((2,)),
            dma(()),
            dma(()),
            dma(()),
            dma((8,)),
            dma(()),
            dma(()),
            dma((4,)),
        ],
        compiler_params=pltpu.CompilerParams(
            collective_id=0, has_side_effects=True, vmem_limit_bytes=56 * 1024 * 1024
        ),
    )(
        gate_param, up_param, gate_grad, up_grad, gate_mom, up_mom, gate_var, up_var,
        q_rows, keys_fresh, vals_fresh, cache_keys, cache_values, lens, res, out_proj, gain,
    )
    return (
        gate_updated,
        up_updated,
        mixed.transpose(1, 0, 2),
        hidden.transpose(1, 0, 2),
    )


def solution(mesh):
    both = P(("dp", "tp"), None)
    group = P("dp", None, "tp")
    return jax.shard_map(
        on_device,
        mesh=mesh,
        in_specs=(both,) * 8 + (group,) * 5 + (P("dp"), group, P("tp", None), P()),
        out_specs=(both, both, group, group),
        check_vma=False,
    )
```

time: 292 us -> 107 us (0.37)
  the two profiles are of different devices: /device:TPU:1 before, /device:TPU:2 now
where the time goes in v1:
time: 107 us
  Pallas kernels  91.6 us (86%)
  local copies, waits for them, and re-layouts  14.5 us (14%)
    pallas_call x1, Pallas kernels, on_device(): pl.pallas_call(kernel, out_shape=(jax.ShapeDtypeStruct((16, FF), BF16), j...  91.6 us
    unnamed x7, local copies, waits for them, and re-layouts  7.51 us

profile of v1, /device:TPU:2, one launch (start us, length us, event | category | flops | bytes accessed | tf_op | source)
XLA Modules:
  0.0 106.7 jit_solution(5250795089576800001)
XLA Ops:
  0.6 1.4 %broadcast_in_dim.2.len_in = s32[32,1,128]{2,1,0:T(1,128)} broadcast(s32[32]{0:T(128)} %param.30), dimensions={0} | broadcast | bytes 16512 | tf_op jit(solution)/shard_map/broadcast_in_dim | solution.py:448
  2.0 1.3 %reshape.18.gain_in = bf16[1,4096]{1,0:T(2,128)(2,1)} reshape(bf16[4096]{0:T(1024)(128)(2,1)} %param.33) | data formatting | bytes 16384 | tf_op jit(solution)/shard_map/reshape | solution.py:450
  3.3 1.5 %reshape.17.q_in = bf16[32,8,128]{2,1,0:T(8,128)(2,1)} reshape(bf16[32,2,512]{2,1,0:T(2,128)(2,1)} %param.25) | data formatting | bytes 131072 | tf_op jit(solution)/shard_map/reshape | solution.py:444
  4.8 1.5 %copy.25 = bf16[32,2,512]{2,0,1:T(8,128)(2,1)} copy(bf16[32,2,512]{2,1,0:T(2,128)(2,1)} %param.31) | data formatting | bytes 131072 | tf_op args[14]
  6.3 1.4 %pad.7.nk_in = bf16[32,16,128]{2,1,0:T(8,128)(2,1)} pad(bf16[32,2,128]{2,1,0:T(2,128)(2,1)} %param.26, bf16[]{:T(256)} %constant.2.clone.1), padding=0_0x0_14x0_0 | pad | bytes 147458 | tf_op jit(solution)/shard_map/jit(_pad)/pad | solution.py:446
  7.7 1.4 %pad.8.nv_in = bf16[32,16,128]{2,1,0:T(8,128)(2,1)} pad(bf16[32,2,128]{2,1,0:T(2,128)(2,1)} %param.27, bf16[]{:T(256)} %constant.2.clone.1), padding=0_0x0_14x0_0 | pad | bytes 147458 | tf_op jit(solution)/shard_map/jit(_pad)/pad | solution.py:447
  9.1 91.6 %shard_map.192 = (bf16[16,14336]{1,0:T(8,128)(2,1)}, bf16[16,14336]{1,0:T(8,128)(2,1)}, bf16[2,32,512]{2,1,0:T(8,128)(2,1)}, bf16[2,32,1792]{2,1,0:T(8,128)(2,1)}) custom-call(bf16[16,14336]{1,0:T(8,128)(2,1)} %gp.1, bf16[16,14336]{1,0:T(8,128)(2,1)} %up.1, bf16[16,14336]{1,0:T(8,128)(2,1)} %gg.1, bf16[16,14336]{1,0:T(8,128)(2,1)} %ug.1, ...), custom_call_target="tpu_custom_call" | custom-call | tf_op jit(solution)/shard_map/pallas_call | solution.py:454
  100.6 0.0 copy-start
  100.6 1.6 %copy.22 = bf16[32,2,512]{2,1,0:T(2,128)(2,1)} copy(bf16[32,2,512]{2,0,1:T(8,128)(2,1)} %bitcast.7) | data formatting | bytes 131072
  102.2 1.9 %copy.23 = bf16[32,2,1792]{2,1,0:T(2,128)(2,1)} copy(bf16[32,2,1792]{2,0,1:T(8,128)(2,1)} %bitcast.6) | data formatting | bytes 458752
  104.1 1.8 %copy.28 = bf16[16,14336]{1,0:T(8,128)(2,1)} copy(bf16[16,14336]{1,0:T(8,128)(2,1)} %get-tuple-element.20) | data formatting | bytes 917504
  105.9 0.0 copy-done
  105.9 0.8 copy.29
Async XLA Ops:
  100.6 5.3 %copy-start = (bf16[16,14336]{1,0:T(8,128)(2,1)S(1)}, bf16[16,14336]{1,0:T(8,128)(2,1)}, u32[]{:S(2)}) copy-start(bf16[16,14336]{1,0:T(8,128)(2,1)} %get-tuple-element.21) | copy-start | bytes 1376260

commit v2 on v1

v2 whole, which is shorter than its diff:
```python
import functools
import math

import jax
import jax.numpy as jnp
from jax import lax
from jax.experimental import pallas as pl
from jax.experimental.pallas import tpu as pltpu
from jax.sharding import PartitionSpec as P

MESH = pl.DeviceIdType.MESH
F32 = jnp.float32
BF16 = jnp.bfloat16

HD = 128
ROWS = 32
SLOTS = 192
PADDED = 208
D = 4096
FF = 14336
NZ, NY = 8, 4
PLANE = NZ * NY
WIDTHS = (256, 256, 384)
CHUNKS = len(WIDTHS)
A2A, X1, X2, CORE, OUT = 0, 3, 6, 9, 12
RES, RS, GATHER, MIX, RING_A, RING_B, SPREAD = range(14, 21)
PAIR = 896

beta_one = 0.9
beta_two = 0.95
adam_step = 20
learn_rate = 0.1
decay_rate = 0.1
epsilon_adam = 1e-08
epsilon_norm = 1e-05
masked_score = -1e30


def adamw_update(param, grad, moment, second):
    grad32 = grad.astype(F32)
    moment_new = beta_one * moment.astype(F32) + (1.0 - beta_one) * grad32
    second_new = beta_two * second.astype(F32) + (1.0 - beta_two) * grad32 * grad32
    corr_one = 1.0 - beta_one**adam_step
    corr_two = 1.0 - beta_two**adam_step
    direction = moment_new * (1.0 / corr_one) / (
        jnp.sqrt(second_new * (1.0 / corr_two)) + epsilon_adam
    )
    param32 = param.astype(F32)
    return param32 - learn_rate * (direction + decay_rate * param32)


def kernel(
    len_in,
    gp, up, gg, ug, gm, um, gv, uv,
    q_in, nk_in, nv_in, ck_in, cv_in, res_in, wo_in, gain_in,
    g_out, u_out, mix_out, hid_out,
    adam, gnew, unew, sbuf0, sbuf1, sbuf2, wbuf0, wbuf1, wbuf2,
    raw, new_raw, raw32, new32, q32, res, kbuf, vbuf, wo, gain,
    ctx32, ctxb, pbuf, rsbuf, rres, ybuf, squares, abuf, bbuf, hbuf, gains,
    load_sem, send_sem, a2a_sem, x1_sem, x2_sem, core_sem,
    rs_sem, res_sem, y_sem, square_sem, za_sem, zb_sem, spread_sem, mix_sem, out_sem, store_sem,
):
    dp = lax.axis_index("dp")
    tp = lax.axis_index("tp")
    x_lo = dp // 16
    z = (dp // 2) % NZ
    c = dp % 2
    y = tp // 2
    h = tp % 2
    x = h * 2 + x_lo
    other = 1 - h

    def place(xx, yy, zz, cc):
        return ((xx % 2) * 16 + zz * 2 + cc, yy * 2 + xx // 2)

    right = (x + 1) % 4
    left = (x + 3) % 4
    across = (x + 2) % 4
    z_up = (z + 1) % NZ
    z_dn = (z + NZ - 1) % NZ

    load_q = pltpu.make_async_copy(q_in, raw.at[0], load_sem.at[8])
    load_res = pltpu.make_async_copy(res_in, raw.at[1], load_sem.at[9])
    load_nk = pltpu.make_async_copy(nk_in, new_raw.at[0], load_sem.at[10])
    load_nv = pltpu.make_async_copy(nv_in, new_raw.at[1], load_sem.at[11])
    load_k = pltpu.make_async_copy(ck_in, kbuf.at[:, pl.ds(0, SLOTS), :], load_sem.at[12])
    load_v = pltpu.make_async_copy(cv_in, vbuf.at[:, pl.ds(0, SLOTS), :], load_sem.at[13])
    load_wo = pltpu.make_async_copy(wo_in, wo, load_sem.at[14])
    load_gain = pltpu.make_async_copy(gain_in, gain, load_sem.at[15])
    for copy in (load_q, load_res, load_nk, load_nv):
        copy.start()
    loads = []
    for i, ref in enumerate((gp, gg, gm, gv, up, ug, um, uv)):
        loads.append(pltpu.make_async_copy(ref, adam.at[i], load_sem.at[i]))
    for copy in loads:
        copy.start()
    for copy in (load_k, load_v, load_wo, load_gain):
        copy.start()

    barrier = pltpu.get_barrier_semaphore()

    def greet(where):
        pl.semaphore_signal(barrier, inc=1, device_id=where, device_id_type=MESH)

    @pl.loop(1, PLANE)
    def _(o):
        greet(place(x, (y + o // NZ) % NY, (z + o % NZ) % NZ, c))

    @pl.loop(1, NZ)
    def _(o):
        greet(place(across, y, (z + o) % NZ, c))

    @pl.loop(0, NY)
    def _(o):
        greet(place(across, (y + o) % NY, z, c))

    greet(place(right, y, z, c))
    greet(place(left, y, z, c))
    greet(place(x, y, z, 1 - c))

    for copy in (load_q, load_res, load_nk, load_nv):
        copy.wait()
    for i in range(2):
        raw32[i] = raw[i].astype(F32)
    for s in range(2):
        for g in range(4):
            q32[:, s * 4 + g, :] = raw32[0, :, s, g * HD : (g + 1) * HD]
        res[s] = raw32[1, :, s, :].astype(BF16)
    for i, buf in enumerate((kbuf, vbuf)):
        new32[...] = jnp.zeros_like(new32)
        new32[:, 0:2, :] = new_raw[i].astype(F32)
        buf[:, SLOTS:PADDED, :] = new32[...].astype(BF16)

    sbufs = (sbuf0, sbuf1, sbuf2)
    wbufs = (wbuf0, wbuf1, wbuf2)

    def remote(src, dst, send, recv, where):
        return pltpu.make_async_remote_copy(
            src_ref=src,
            dst_ref=dst,
            send_sem=send,
            recv_sem=recv,
            device_id=where,
            device_id_type=MESH,
        )

    for copy in loads:
        copy.wait()
    pl.semaphore_wait(barrier, PLANE - 1 + NZ - 1 + NY + 3)
    position = y * NZ + z

    def updated(start, width):
        cols = pl.ds(pl.multiple_of(start, 128), width)
        tiles = []
        for first, dest in ((0, gnew), (4, unew)):
            value = adamw_update(
                adam[first, :, cols],
                adam[first + 1, :, cols],
                adam[first + 2, :, cols],
                adam[first + 3, :, cols],
            )
            dest[:, cols] = value.astype(BF16)
            tiles.append([value[:, i * 128 : (i + 1) * 128] for i in range(width // 128)])
        return tiles

    def fill(dest, tiles):
        for i, tile in enumerate(tiles):
            dest[:, i * 128 : (i + 1) * 128] = tile.astype(BF16)

    def send_block(q, dest):
        remote(
            sbufs[q].at[dest],
            wbufs[q].at[x_lo, z, c, y, h],
            send_sem.at[A2A + q],
            a2a_sem.at[q],
            place(x, dest // NZ, dest % NZ, c),
        ).start()

    def first_chunks(dest):
        gate, upper = updated((dest // 2) * PAIR + (dest % 2) * 512, 256)
        fill(sbuf0.at[dest], (gate[0], upper[0]))
        fill(sbuf1.at[dest], (gate[1], upper[1]))

    @pl.loop(1, PLANE)
    def _(t):
        dest = (position + t) % PLANE
        first_chunks(dest)
        send_block(0, dest)

    @pl.loop(1, PLANE)
    def _(t):
        send_block(1, (position + t) % PLANE)

    first_chunks(position)
    wbuf0[x_lo, z, c, y, h] = sbuf0[position]
    wbuf1[x_lo, z, c, y, h] = sbuf1[position]

    def last_chunk(pair):
        gate, upper = updated(pair * PAIR + 256, 256)
        last_gate, last_upper = updated(pair * PAIR + 768, 128)
        lane = lax.broadcasted_iota(jnp.int32, (16, 128), 1)
        turned = pltpu.roll(upper[1], 64, 1)
        even = jnp.where(lane < 64, gate[1], turned)
        odd = jnp.where(lane < 64, turned, gate[1])
        fill(sbuf2.at[2 * pair], (gate[0], upper[0], even))
        fill(sbuf2.at[2 * pair + 1], (last_gate[0], last_upper[0], odd))

    to_across = place(across, y, z, c)
    res_copy = remote(res.at[other], rres.at[h], send_sem.at[RES], res_sem, to_across)
    res_copy.start()
    rres[h] = res[h]

    load_k.wait()
    load_v.wait()
    part = 8

    @pl.loop(0, ROWS // part)
    def _(i):
        rows = pl.ds(pl.multiple_of(i * part, part), part)
        slot = lax.broadcasted_iota(jnp.int32, (part, 8, PADDED), 2)
        token = lax.broadcasted_iota(jnp.int32, (part, 8, PADDED), 1) // 4
        scores = lax.dot_general(
            q32[rows].astype(BF16), kbuf[rows], (((2,), (2,)), ((0,), (0,))), preferred_element_type=F32
        ) * (1.0 / math.sqrt(HD))
        filled = jnp.concatenate(
            [jnp.full((1, 8, PADDED), len_in[i * part + k], jnp.int32) for k in range(part)], axis=0
        )
        fresh = (slot >= SLOTS) & (slot <= SLOTS + token)
        scores = jnp.where((slot < filled) | fresh, scores, masked_score)
        expo = jnp.exp(scores - jnp.max(scores, axis=-1, keepdims=True))
        weights = (expo / jnp.sum(expo, axis=-1, keepdims=True)).astype(BF16)
        context = lax.dot_general(
            weights, vbuf[rows], (((2,), (1,)), ((0,), (0,))), preferred_element_type=F32
        )
        ctx32[rows] = context

    for s in range(2):
        for g in range(4):
            ctxb[s * ROWS : (s + 1) * ROWS, g * HD : (g + 1) * HD] = ctx32[:, s * 4 + g, :].astype(BF16)

    def held(q, xx):
        return wbufs[q].at[xx % 2, :, c, :, xx // 2]

    def held_half(q, xx, half):
        return wbufs[q].at[xx % 2, pl.ds(half * 4, 4), c, :, xx // 2]

    def wait_a2a(q):
        some = sbufs[q].at[pl.ds(0, PLANE - 1)]
        remote(some, some, send_sem.at[A2A + q], a2a_sem.at[q], to_across).wait_recv()

    to_right = place(right, y, z, c)
    to_left = place(left, y, z, c)
    to_twin = place(x, y, z, 1 - c)

    def stage_one(q):
        mine = held(q, x)
        for side, where in enumerate((to_right, to_left)):
            remote(mine, mine, send_sem.at[X1 + q], x1_sem.at[2 * q + side], where).start()
        remote(mine, mine, send_sem.at[CORE + q], core_sem.at[q], to_twin).start()

    def stage_two(q):
        from_left, from_right = held(q, left), held(q, right)
        remote(from_left, from_left, send_sem.at[X1 + q], x1_sem.at[2 * q], to_right).wait_recv()
        half = held_half(q, left, 0)
        remote(half, half, send_sem.at[X2 + q], x2_sem.at[2 * q], to_right).start()
        remote(from_right, from_right, send_sem.at[X1 + q], x1_sem.at[2 * q + 1], to_left).wait_recv()
        half = held_half(q, right, 1)
        remote(half, half, send_sem.at[X2 + q], x2_sem.at[2 * q + 1], to_left).start()
        for part in (from_left, from_right):
            remote(part, part, send_sem.at[CORE + q], core_sem.at[q], to_twin).start()

    def stage_three(q):
        for side in range(2):
            half = held_half(q, across, side)
            remote(half, half, send_sem.at[X2 + q], x2_sem.at[2 * q + side], to_right).wait_recv()
        part = held(q, across)
        remote(part, part, send_sem.at[CORE + q], core_sem.at[q], to_twin).start()

    wait_a2a(0)
    stage_one(0)

    load_wo.wait()

    @pl.loop(0, 8)
    def _(j):
        cols = pl.ds(pl.multiple_of(j * 512, 512), 512)
        partial = jnp.dot(ctxb[...], wo[:, cols], preferred_element_type=F32).astype(BF16)
        pbuf[j, 0] = partial[:ROWS]
        pbuf[j, 1] = partial[ROWS:]

    @pl.loop(1, 8)
    def _(o):
        yy = (y + o // 2) % NY
        hh = (h + o) % 2
        remote(
            pbuf.at[pl.ds(2 * yy, 2), hh],
            rsbuf.at[tp],
            send_sem.at[RS],
            rs_sem,
            place(hh * 2 + x_lo, yy, z, c),
        ).start()

    rsbuf[tp] = pbuf[pl.ds(2 * y, 2), h]

    @pl.loop(1, 16)
    def _(t):
        pair = (position // 2 + t) % 16
        last_chunk(pair)
        send_block(2, 2 * pair)
        send_block(2, 2 * pair + 1)

    last_chunk(position // 2)
    send_block(2, position + 1 - 2 * (position % 2))
    wbuf2[x_lo, z, c, y, h] = sbuf2[position]
    store_g = pltpu.make_async_copy(gnew, g_out, store_sem.at[0])
    store_u = pltpu.make_async_copy(unew, u_out, store_sem.at[1])
    store_g.start()
    store_u.start()

    wait_a2a(1)
    stage_one(1)

    some = rsbuf.at[pl.ds(0, 7)]
    remote(some, some, send_sem.at[RS], rs_sem, to_across).wait_recv()
    remote(res.at[0], rres.at[0], send_sem.at[RES], res_sem, to_across).wait_recv()
    square = jnp.zeros((ROWS, 1), F32)
    for k in range(2):
        total = rsbuf[0, k].astype(F32)
        for i in range(1, 8):
            total = total + rsbuf[i, k].astype(F32)
        ybuf[2 * y + k] = (rres[k].astype(F32) + total).astype(BF16)
        value = ybuf[2 * y + k].astype(F32)
        square = square + jnp.sum(value * value, axis=-1, keepdims=True)
    squares[y] = jnp.broadcast_to(square, (ROWS, 128))

    y_peers = [place(x, (y + o) % NY, z, c) for o in range(1, NY)]
    for where in y_peers:
        remote(squares.at[y], squares.at[y], send_sem.at[GATHER], square_sem, where).start()
    for where in y_peers:
        mine = ybuf.at[2 * y]
        remote(mine, mine, send_sem.at[GATHER], y_sem, where).start()
    remote(ybuf.at[2 * y + other], mix_out.at[h], send_sem.at[MIX], mix_sem, to_across).start()
    store_mix = pltpu.make_async_copy(ybuf.at[2 * y + h], mix_out.at[h], store_sem.at[2])
    store_mix.start()
    load_gain.wait()
    gain32 = gain[...].astype(F32).reshape(1, D)
    for j in range(8):
        gains[j] = gain32[:, j * 512 : (j + 1) * 512]
    some = squares.at[pl.ds(0, 3)]
    remote(some, some, send_sem.at[GATHER], square_sem, to_across).wait_recv()
    square = (squares[0] + squares[1] + squares[2] + squares[3])[:, 0:1]
    factor = lax.rsqrt(square * (1.0 / D) + epsilon_norm)
    bbuf[z, y] = (ybuf[2 * y + 1].astype(F32) * factor * gains[2 * y + 1]).astype(BF16)

    to_up = place(x, y, z_up, c)
    to_dn = place(x, y, z_dn, c)

    def ring(kind, step, up_ref, dn_ref):
        sems = zb_sem if kind == RING_B else za_sem
        remote(up_ref, up_ref, send_sem.at[kind], sems.at[2 * step], to_up).start()
        remote(dn_ref, dn_ref, send_sem.at[kind], sems.at[2 * step + 1], to_dn).start()

    def ring_wait(kind, step, up_ref, dn_ref):
        sems = zb_sem if kind == RING_B else za_sem
        remote(up_ref, up_ref, send_sem.at[kind], sems.at[2 * step], to_up).wait_recv()
        remote(dn_ref, dn_ref, send_sem.at[kind], sems.at[2 * step + 1], to_dn).wait_recv()

    def block(shift):
        return abuf.at[(z + NZ + shift) % NZ]

    def block_b(shift):
        return bbuf.at[(z + NZ + shift) % NZ, y]

    def spread(shift):
        for where in y_peers:
            part = block_b(shift)
            remote(part, part, send_sem.at[SPREAD], spread_sem, where).start()

    low, high = pl.ds(0, 16), pl.ds(16, 16)
    ring(RING_B, 0, block_b(0), block_b(0))
    spread(0)
    some = ybuf.at[pl.ds(0, 3)]
    remote(some, some, send_sem.at[GATHER], y_sem, to_across).wait_recv()
    for k in range(4):
        abuf[z, :, k * 512 : (k + 1) * 512] = (
            ybuf[2 * k].astype(F32) * factor * gains[2 * k]
        ).astype(BF16)
    ring(RING_A, 0, block(0), block(0))
    ring_wait(RING_B, 0, block_b(-1), block_b(1))
    ring(RING_B, 1, block_b(-1), block_b(1))
    spread(-1)
    spread(1)
    stage_two(0)
    ring_wait(RING_B, 1, block_b(-2), block_b(2))
    ring(RING_B, 2, block_b(-2), block_b(2))
    spread(-2)
    spread(2)
    wait_a2a(2)
    stage_one(2)
    ring_wait(RING_A, 0, block(-1), block(1))
    ring(RING_A, 1, block(-1), block(1))
    ring_wait(RING_B, 2, block_b(-3), block_b(3))
    ring(RING_B, 3, block_b(-3).at[low], block_b(3).at[high])
    spread(-3)
    spread(3)
    stage_two(1)
    stage_three(0)
    ring_wait(RING_A, 1, block(-2), block(2))
    ring(RING_A, 2, block(-2), block(2))
    ring_wait(RING_B, 3, block_b(4).at[low], block_b(4).at[high])
    spread(4)
    stage_three(1)
    ring_wait(RING_A, 2, block(-3), block(3))
    ring(RING_A, 3, block(-3).at[low], block(3).at[high])
    stage_two(2)
    ring_wait(RING_A, 3, block(4).at[low], block(4).at[high])
    some = abuf.at[pl.ds(0, 6)]
    remote(some, some, send_sem.at[SPREAD], spread_sem, to_across).wait_recv()

    def core_wait(q):
        both = wbufs[q].at[:, :, 1 - c]
        remote(both, both, send_sem.at[CORE + q], core_sem.at[q], to_twin).wait_recv()

    scale = 1.0 / math.sqrt(D)

    def product(q):
        acts = jnp.zeros((NZ * ROWS, WIDTHS[q]), F32)
        for j in range(8):
            if j % 2 == 0:
                left_side = abuf[:, :, j * 256 : j * 256 + 512]
            else:
                left_side = bbuf[:, j // 2]
            first = (j % 4) * 2
            right_side = wbufs[q][j // 4, first : first + 2].reshape(512, WIDTHS[q])
            acts = acts + jnp.dot(
                left_side.reshape(NZ * ROWS, 512), right_side, preferred_element_type=F32
            )
        return acts * scale

    def gated(gate, upper):
        value = gate / (1.0 + jnp.exp(-gate)) * upper
        return value.astype(BF16).reshape(NZ, ROWS, 128)

    owner = (z // 4) * 2 + x_lo
    stays = z // 4 == h

    def send_hidden(q):
        @pl.loop(1, NZ)
        def _(o):
            zz = (z + o) % NZ
            remote(
                hbuf.at[q, zz],
                hid_out.at[q, h, z % 4],
                send_sem.at[OUT + q],
                out_sem.at[q],
                place(owner, y, zz, c),
            ).start()

        @pl.when(stays)
        def _():
            pltpu.make_async_copy(hbuf.at[q, z], hid_out.at[q, h, z % 4], out_sem.at[q]).start()

        @pl.when(jnp.logical_not(stays))
        def _():
            remote(
                hbuf.at[q, z],
                hid_out.at[q, h, z % 4],
                send_sem.at[OUT + q],
                out_sem.at[q],
                to_across,
            ).start()

    core_wait(0)
    acts = product(0)
    hbuf[0, :, :, 0:128] = gated(acts[:, 0:128], acts[:, 128:256])
    core_wait(1)
    acts = product(1)
    hbuf[0, :, :, 128:256] = gated(acts[:, 0:128], acts[:, 128:256])
    send_hidden(0)
    stage_three(2)
    core_wait(2)
    acts = product(2)
    hbuf[1, :, :, 0:128] = gated(acts[:, 0:128], acts[:, 128:256])
    hbuf[1, :, :, 128:256] = gated(acts[:, 256:384], pltpu.roll(acts[:, 256:384], 64, 1))
    send_hidden(1)

    remote(mix_out.at[0], mix_out.at[0], send_sem.at[MIX], mix_sem, to_across).wait_recv()
    for q in range(2):
        whole = hid_out.at[q]
        remote(whole, whole, send_sem.at[OUT + q], out_sem.at[q], to_across).wait_recv()

    def sent(index, ref):
        remote(ref, ref, send_sem.at[index], mix_sem, to_across).wait_send()

    for q in range(CHUNKS):
        sent(A2A + q, sbufs[q].at[pl.ds(0, PLANE - 1)])
        for _ in range(2):
            sent(X1 + q, held(q, x))
        for _ in range(2):
            sent(X2 + q, held_half(q, left, 0))
        sent(CORE + q, wbufs[q].at[:, :, c])
    sent(RES, res.at[0])
    sent(RS, rsbuf.at[pl.ds(0, 7)])
    sent(GATHER, squares.at[pl.ds(0, 3)])
    sent(GATHER, ybuf.at[pl.ds(0, 3)])
    sent(MIX, ybuf.at[0])
    sent(RING_A, abuf.at[pl.ds(0, 7)])
    sent(RING_B, bbuf.at[pl.ds(0, 7), 0])
    sent(SPREAD, abuf.at[pl.ds(0, 6)])
    for q in range(2):
        sent(OUT + q, hbuf.at[q, pl.ds(0, 7)])

    @pl.when(jnp.logical_not(stays))
    def _():
        for q in range(2):
            sent(OUT + q, hbuf.at[q, 0])

    store_g.wait()
    store_u.wait()
    store_mix.wait()


def finish(
    g_in, u_in, mix_in, hid_in, g_out, u_out, mix_out, hid_out, shards, mix32, hid32, sem
):
    halves = [pl.ds(0, FF // 2), pl.ds(FF // 2, FF // 2)]
    load, store = [], []
    for i, (source, dest) in enumerate(((g_in, g_out), (u_in, u_out))):
        for k, cols in enumerate(halves):
            held = shards.at[i, :, cols]
            load.append(pltpu.make_async_copy(source.at[:, cols], held, sem.at[2 * i + k]))
            store.append(pltpu.make_async_copy(held, dest.at[:, cols], sem.at[4 + 2 * i + k]))
    for copy in load:
        copy.start()
    lane = lax.broadcasted_iota(jnp.int32, (ROWS, 128), 1)
    for s in range(2):
        mix32[:, s, :] = mix_in[s].astype(F32)
        for p in range(2):
            even, odd = 2 * p, 2 * p + 1
            base = p * PAIR
            middle = jnp.where(
                lane < 64,
                hid_in[1, s, even, :, 128:256].astype(F32),
                hid_in[1, s, odd, :, 128:256].astype(F32),
            )
            hid32[:, s, base : base + 256] = hid_in[0, s, even].astype(F32)
            hid32[:, s, base + 256 : base + 384] = hid_in[1, s, even, :, 0:128].astype(F32)
            hid32[:, s, base + 384 : base + 512] = middle
            hid32[:, s, base + 512 : base + 768] = hid_in[0, s, odd].astype(F32)
            hid32[:, s, base + 768 : base + 896] = hid_in[1, s, odd, :, 0:128].astype(F32)
    for first, second in zip(load, store):
        first.wait()
        second.start()
    mix_out[...] = mix32[...].astype(BF16)
    hid_out[...] = hid32[...].astype(BF16)
    for copy in store:
        copy.wait()


def on_device(
    gate_param,
    up_param,
    gate_grad,
    up_grad,
    gate_mom,
    up_mom,
    gate_var,
    up_var,
    queries,
    new_keys,
    new_values,
    cache_keys,
    cache_values,
    cache_len,
    residual,
    out_proj,
    norm_gain,
):
    dma = pltpu.SemaphoreType.DMA
    vmem = pltpu.VMEM
    anywhere = pl.BlockSpec(memory_space=pl.ANY)
    inside = pl.BlockSpec(memory_space=vmem)
    shard = jax.ShapeDtypeStruct((16, FF), BF16)
    gate_updated, up_updated, mixed, hidden = pl.pallas_call(
        kernel,
        out_shape=(
            shard,
            shard,
            jax.ShapeDtypeStruct((2, ROWS, 512), BF16),
            jax.ShapeDtypeStruct((2, 2, 4, ROWS, 256), BF16),
        ),
        in_specs=[pl.BlockSpec(memory_space=pltpu.SMEM)] + [anywhere] * 16,
        out_specs=[anywhere] * 4,
        scratch_shapes=[
            vmem((8, 16, FF), BF16),
            vmem((16, FF), BF16),
            vmem((16, FF), BF16),
            *[vmem((PLANE, 16, width), BF16) for width in WIDTHS],
            *[vmem((2, NZ, 2, NY, 2, 16, width), BF16) for width in WIDTHS],
            vmem((2, ROWS, 2, 512), BF16),
            vmem((2, ROWS, 2, HD), BF16),
            vmem((2, ROWS, 2, 512), F32),
            vmem((ROWS, 16, HD), F32),
            vmem((ROWS, 8, HD), F32),
            vmem((2, ROWS, 512), BF16),
            vmem((ROWS, PADDED, HD), BF16),
            vmem((ROWS, PADDED, HD), BF16),
            vmem((512, D), BF16),
            vmem((D,), BF16),
            vmem((ROWS, 8, HD), F32),
            vmem((2 * ROWS, 512), BF16),
            vmem((8, 2, ROWS, 512), BF16),
            vmem((8, 2, ROWS, 512), BF16),
            vmem((2, ROWS, 512), BF16),
            vmem((8, ROWS, 512), BF16),
            vmem((NY, ROWS, 128), F32),
            vmem((NZ, ROWS, D // 2), BF16),
            vmem((NZ, NY, ROWS, 512), BF16),
            vmem((2, NZ, ROWS, 256), BF16),
            vmem((8, 1, 512), F32),
            dma((16,)),
            dma((21,)),
            dma((CHUNKS,)),
            dma((2 * CHUNKS,)),
            dma((2 * CHUNKS,)),
            dma((CHUNKS,)),
            dma(()),
            dma(()),
            dma(()),
            dma(()),
            dma((8,)),
            dma((8,)),
            dma(()),
            dma(()),
            dma((2,)),
            dma((3,)),
        ],
        compiler_params=pltpu.CompilerParams(
            collective_id=0, has_side_effects=True, vmem_limit_bytes=56 * 1024 * 1024
        ),
    )(
        cache_len,
        gate_param, up_param, gate_grad, up_grad, gate_mom, up_mom, gate_var, up_var,
        queries, new_keys, new_values, cache_keys, cache_values, residual, out_proj, norm_gain,
    )
    return pl.pallas_call(
        finish,
        out_shape=(
            shard,
            shard,
            jax.ShapeDtypeStruct((ROWS, 2, 512), BF16),
            jax.ShapeDtypeStruct((ROWS, 2, 1792), BF16),
        ),
        in_specs=[anywhere, anywhere, inside, inside],
        out_specs=(anywhere, anywhere, inside, inside),
        scratch_shapes=[
            vmem((2, 16, FF), BF16),
            vmem((ROWS, 2, 512), F32),
            vmem((ROWS, 2, 1792), F32),
            dma((8,)),
        ],
        compiler_params=pltpu.CompilerParams(vmem_limit_bytes=56 * 1024 * 1024),
    )(gate_updated, up_updated, mixed, hidden)


def solution(mesh):
    both = P(("dp", "tp"), None)
    group = P("dp", None, "tp")
    return jax.shard_map(
        on_device,
        mesh=mesh,
        in_specs=(both,) * 8 + (group,) * 5 + (P("dp"), group, P("tp", None), P()),
        out_specs=(both, both, group, group),
        check_vma=False,
    )
```

time: 107 us -> 81.3 us (0.76)
  the two profiles are of different devices: /device:TPU:2 before, /device:TPU:1 now
where the time goes in v2:
time: 81.3 us; the launch traced here: 81.2 us
  Pallas kernels  80.5 us (99%)
    pallas_call x1, Pallas kernels, on_device(): pl.pallas_call(kernel, out_shape=(shard, shard, jax.ShapeDtypeStruct((2,...  76.8 us
    pallas_call x1, Pallas kernels, on_device(): pl.pallas_call(finish, out_shape=(shard, shard, jax.ShapeDtypeStruct((ROW...  3.74 us

profile of v2, /device:TPU:1, one launch (start us, length us, event | category | flops | bytes accessed | tf_op | source)
XLA Modules:
  0.0 81.2 jit_solution(15264999662756770640)
XLA Ops:
  0.6 76.8 %shard_map.192 = (bf16[16,14336]{1,0:T(8,128)(2,1)}, bf16[16,14336]{1,0:T(8,128)(2,1)}, bf16[2,32,512]{2,1,0:T(8,128)(2,1)}, bf16[2,2,4,32,256]{4,3,2,1,0:T(8,128)(2,1)}) custom-call(s32[32]{0:T(128)} %len_in.1, bf16[16,14336]{1,0:T(8,128)(2,1)} %gp.1, bf16[16,14336]{1,0:T(8,128)(2,1)} %up.1, bf16[16,14336]{1,0:T(8,128)(2,1)} %gg.1, bf16[16,14336]{1,0:T(8,128)(2,1)} %ug.1, ...), custom_call_target="tpu_custom_call" | custom-call | tf_op jit(solution)/shard_map/pallas_call | solution.py:584
  77.5 3.7 %shard_map.193 = (bf16[16,14336]{1,0:T(8,128)(2,1)}, bf16[16,14336]{1,0:T(8,128)(2,1)}, bf16[32,2,512]{2,1,0:T(2,128)(2,1)}, bf16[32,2,1792]{2,1,0:T(2,128)(2,1)}) custom-call(bf16[16,14336]{1,0:T(8,128)(2,1)} %get-tuple-element.8.g_in, bf16[16,14336]{1,0:T(8,128)(2,1)} %get-tuple-element.9.u_in, bf16[2,32,512]{2,1,0:T(8,128)(2,1)} %get-tuple-element.10.mix_in, ...), custom_call_target="tpu_custom_call" | custom-call | tf_op jit(solution)/shard_map/pallas_call | solution.py:646

commit v3 on v2

--- a/solution.py
+++ b/solution.py
@@ -23,7 +23,7 @@
 WIDTHS = (256, 256, 384)
 CHUNKS = len(WIDTHS)
 A2A, X1, X2, CORE, OUT = 0, 3, 6, 9, 12
-RES, RS, GATHER, MIX, RING_A, RING_B, SPREAD = range(14, 21)
+RES, RS, GATHER, MIX, SPREAD, RING = range(14, 20)
 PAIR = 896
 
 beta_one = 0.9
@@ -58,7 +58,7 @@
     raw, new_raw, raw32, new32, q32, res, kbuf, vbuf, wo, gain,
     ctx32, ctxb, pbuf, rsbuf, rres, ybuf, squares, abuf, bbuf, hbuf, gains,
     load_sem, send_sem, a2a_sem, x1_sem, x2_sem, core_sem,
-    rs_sem, res_sem, y_sem, square_sem, za_sem, zb_sem, spread_sem, mix_sem, out_sem, store_sem,
+    rs_sem, res_sem, y_sem, square_sem, z_sem, spread_sem, mix_sem, out_sem, store_sem,
 ):
     dp = lax.axis_index("dp")
     tp = lax.axis_index("tp")
@@ -276,9 +276,6 @@
         part = held(q, across)
         remote(part, part, send_sem.at[CORE + q], core_sem.at[q], to_twin).start()
 
-    wait_a2a(0)
-    stage_one(0)
-
     load_wo.wait()
 
     @pl.loop(0, 8)
@@ -317,8 +314,8 @@
     store_g.start()
     store_u.start()
 
-    wait_a2a(1)
-    stage_one(1)
+    wait_a2a(0)
+    stage_one(0)
 
     some = rsbuf.at[pl.ds(0, 7)]
     remote(some, some, send_sem.at[RS], rs_sem, to_across).wait_recv()
@@ -342,6 +339,8 @@
     remote(ybuf.at[2 * y + other], mix_out.at[h], send_sem.at[MIX], mix_sem, to_across).start()
     store_mix = pltpu.make_async_copy(ybuf.at[2 * y + h], mix_out.at[h], store_sem.at[2])
     store_mix.start()
+    wait_a2a(1)
+    stage_one(1)
     load_gain.wait()
     gain32 = gain[...].astype(F32).reshape(1, D)
     for j in range(8):
@@ -355,66 +354,81 @@
     to_up = place(x, y, z_up, c)
     to_dn = place(x, y, z_dn, c)
 
-    def ring(kind, step, up_ref, dn_ref):
-        sems = zb_sem if kind == RING_B else za_sem
-        remote(up_ref, up_ref, send_sem.at[kind], sems.at[2 * step], to_up).start()
-        remote(dn_ref, dn_ref, send_sem.at[kind], sems.at[2 * step + 1], to_dn).start()
-
-    def ring_wait(kind, step, up_ref, dn_ref):
-        sems = zb_sem if kind == RING_B else za_sem
-        remote(up_ref, up_ref, send_sem.at[kind], sems.at[2 * step], to_up).wait_recv()
-        remote(dn_ref, dn_ref, send_sem.at[kind], sems.at[2 * step + 1], to_dn).wait_recv()
-
-    def block(shift):
-        return abuf.at[(z + NZ + shift) % NZ]
-
-    def block_b(shift):
-        return bbuf.at[(z + NZ + shift) % NZ, y]
+    def block(chain, shift):
+        zz = (z + NZ + shift) % NZ
+        return bbuf.at[zz, y] if chain == 2 else abuf.at[chain, zz]
+
+    to_side = (to_up, to_dn)
+
+    def ring_copy(chain, step, side, part):
+        return remote(
+            part, part, send_sem.at[RING + chain], z_sem.at[chain * 8 + step * 2 + side], to_side[side]
+        )
+
+    def ring_part(chain, step, side):
+        part = block(chain, (-step, step)[side])
+        return part.at[pl.ds(side * 16, 16)] if step == 3 else part
+
+    def ring_send(chain, step, side):
+        ring_copy(chain, step, side, ring_part(chain, step, side)).start()
+
+    def ring_take(chain, step, side):
+        shift = (-step - 1, step + 1)[side]
+        part = block(chain, shift)
+        if step == 3:
+            part = part.at[pl.ds(side * 16, 16)]
+        ring_copy(chain, step, side, part).wait_recv()
 
     def spread(shift):
         for where in y_peers:
-            part = block_b(shift)
+            part = block(2, shift)
             remote(part, part, send_sem.at[SPREAD], spread_sem, where).start()
 
-    low, high = pl.ds(0, 16), pl.ds(16, 16)
-    ring(RING_B, 0, block_b(0), block_b(0))
+    def advance(chain, step):
+        for side in range(2):
+            ring_take(chain, step, side)
+            if step < 3:
+                ring_send(chain, step + 1, side)
+        if chain == 2:
+            if step < 3:
+                spread(-step - 1)
+                spread(step + 1)
+            else:
+                spread(4)
+
+    for side in range(2):
+        ring_send(2, 0, side)
     spread(0)
     some = ybuf.at[pl.ds(0, 3)]
     remote(some, some, send_sem.at[GATHER], y_sem, to_across).wait_recv()
-    for k in range(4):
-        abuf[z, :, k * 512 : (k + 1) * 512] = (
-            ybuf[2 * k].astype(F32) * factor * gains[2 * k]
-        ).astype(BF16)
-    ring(RING_A, 0, block(0), block(0))
-    ring_wait(RING_B, 0, block_b(-1), block_b(1))
-    ring(RING_B, 1, block_b(-1), block_b(1))
-    spread(-1)
-    spread(1)
+    for chain in range(2):
+        for k in range(2):
+            j = 4 * chain + 2 * k
+            abuf[chain, z, :, k * 512 : (k + 1) * 512] = (
+                ybuf[j].astype(F32) * factor * gains[j]
+            ).astype(BF16)
+        for side in range(2):
+            ring_send(chain, 0, side)
     stage_two(0)
-    ring_wait(RING_B, 1, block_b(-2), block_b(2))
-    ring(RING_B, 2, block_b(-2), block_b(2))
-    spread(-2)
-    spread(2)
+    advance(2, 0)
+    advance(0, 0)
+    advance(1, 0)
+    advance(2, 1)
     wait_a2a(2)
     stage_one(2)
-    ring_wait(RING_A, 0, block(-1), block(1))
-    ring(RING_A, 1, block(-1), block(1))
-    ring_wait(RING_B, 2, block_b(-3), block_b(3))
-    ring(RING_B, 3, block_b(-3).at[low], block_b(3).at[high])
-    spread(-3)
-    spread(3)
+    advance(0, 1)
+    advance(1, 1)
+    advance(2, 2)
     stage_two(1)
+    advance(0, 2)
+    advance(1, 2)
+    advance(2, 3)
     stage_three(0)
-    ring_wait(RING_A, 1, block(-2), block(2))
-    ring(RING_A, 2, block(-2), block(2))
-    ring_wait(RING_B, 3, block_b(4).at[low], block_b(4).at[high])
-    spread(4)
+    advance(0, 3)
+    advance(1, 3)
+    stage_two(2)
     stage_three(1)
-    ring_wait(RING_A, 2, block(-3), block(3))
-    ring(RING_A, 3, block(-3).at[low], block(3).at[high])
-    stage_two(2)
-    ring_wait(RING_A, 3, block(4).at[low], block(4).at[high])
-    some = abuf.at[pl.ds(0, 6)]
+    some = abuf.at[:, pl.ds(0, 6)]
     remote(some, some, send_sem.at[SPREAD], spread_sem, to_across).wait_recv()
 
     def core_wait(q):
@@ -427,7 +441,7 @@
         acts = jnp.zeros((NZ * ROWS, WIDTHS[q]), F32)
         for j in range(8):
             if j % 2 == 0:
-                left_side = abuf[:, :, j * 256 : j * 256 + 512]
+                left_side = abuf[j // 4, :, :, (j % 4) * 256 : (j % 4) * 256 + 512]
             else:
                 left_side = bbuf[:, j // 2]
             first = (j % 4) * 2
@@ -504,9 +518,10 @@
     sent(GATHER, squares.at[pl.ds(0, 3)])
     sent(GATHER, ybuf.at[pl.ds(0, 3)])
     sent(MIX, ybuf.at[0])
-    sent(RING_A, abuf.at[pl.ds(0, 7)])
-    sent(RING_B, bbuf.at[pl.ds(0, 7), 0])
-    sent(SPREAD, abuf.at[pl.ds(0, 6)])
+    for chain in range(2):
+        sent(RING + chain, abuf.at[chain, pl.ds(0, 7)])
+    sent(RING + 2, bbuf.at[pl.ds(0, 7), 0])
+    sent(SPREAD, abuf.at[:, pl.ds(0, 6)])
     for q in range(2):
         sent(OUT + q, hbuf.at[q, pl.ds(0, 7)])
 
@@ -614,12 +629,12 @@
             vmem((2, ROWS, 512), BF16),
             vmem((8, ROWS, 512), BF16),
             vmem((NY, ROWS, 128), F32),
-            vmem((NZ, ROWS, D // 2), BF16),
+            vmem((2, NZ, ROWS, D // 4), BF16),
             vmem((NZ, NY, ROWS, 512), BF16),
             vmem((2, NZ, ROWS, 256), BF16),
             vmem((8, 1, 512), F32),
             dma((16,)),
-            dma((21,)),
+            dma((22,)),
             dma((CHUNKS,)),
             dma((2 * CHUNKS,)),
             dma((2 * CHUNKS,)),
@@ -628,8 +643,7 @@
             dma(()),
             dma(()),
             dma(()),
-            dma((8,)),
-            dma((8,)),
+            dma((24,)),
             dma(()),
             dma(()),
             dma((2,)),

time: 81.3 us -> 75 us (0.923)
  Pallas kernels: 80.5 us -> 74.2 us
    pallas_call x1, Pallas kernels: 76.8 us -> 70.5 us  [on_device(): pl.pallas_call(kernel, out_shape=(shard, shard, jax.ShapeDtypeStruct((2,...]
where the time goes in v3:
time: 75 us; the launch traced here: 74.9 us
  Pallas kernels  74.2 us (99%)
    pallas_call x1, Pallas kernels, on_device(): pl.pallas_call(kernel, out_shape=(shard, shard, jax.ShapeDtypeStruct((2,...  70.5 us
    pallas_call x1, Pallas kernels, on_device(): pl.pallas_call(finish, out_shape=(shard, shard, jax.ShapeDtypeStruct((ROW...  3.74 us

profile of v3, /device:TPU:1, one launch (start us, length us, event | category | flops | bytes accessed | tf_op | source)
XLA Modules:
  0.0 74.9 jit_solution(15061118627221362754)
XLA Ops:
  0.6 70.5 %shard_map.192 = (bf16[16,14336]{1,0:T(8,128)(2,1)}, bf16[16,14336]{1,0:T(8,128)(2,1)}, bf16[2,32,512]{2,1,0:T(8,128)(2,1)}, bf16[2,2,4,32,256]{4,3,2,1,0:T(8,128)(2,1)}) custom-call(s32[32]{0:T(128)} %len_in.1, bf16[16,14336]{1,0:T(8,128)(2,1)} %gp.1, bf16[16,14336]{1,0:T(8,128)(2,1)} %up.1, bf16[16,14336]{1,0:T(8,128)(2,1)} %gg.1, bf16[16,14336]{1,0:T(8,128)(2,1)} %ug.1, ...), custom_call_target="tpu_custom_call" | custom-call | tf_op jit(solution)/shard_map/pallas_call | solution.py:599
  71.2 3.7 %shard_map.193 = (bf16[16,14336]{1,0:T(8,128)(2,1)}, bf16[16,14336]{1,0:T(8,128)(2,1)}, bf16[32,2,512]{2,1,0:T(2,128)(2,1)}, bf16[32,2,1792]{2,1,0:T(2,128)(2,1)}) custom-call(bf16[16,14336]{1,0:T(8,128)(2,1)} %get-tuple-element.8.g_in, bf16[16,14336]{1,0:T(8,128)(2,1)} %get-tuple-element.9.u_in, bf16[2,32,512]{2,1,0:T(8,128)(2,1)} %get-tuple-element.10.mix_in, ...), custom_call_target="tpu_custom_call" | custom-call | tf_op jit(solution)/shard_map/pallas_call | solution.py:660

commit v4 on v3

--- a/solution.py
+++ b/solution.py
@@ -299,6 +299,9 @@
 
     rsbuf[tp] = pbuf[pl.ds(2 * y, 2), h]
 
+    wait_a2a(0)
+    stage_one(0)
+
     @pl.loop(1, 16)
     def _(t):
         pair = (position // 2 + t) % 16
@@ -313,9 +316,6 @@
     store_u = pltpu.make_async_copy(unew, u_out, store_sem.at[1])
     store_g.start()
     store_u.start()
-
-    wait_a2a(0)
-    stage_one(0)
 
     some = rsbuf.at[pl.ds(0, 7)]
     remote(some, some, send_sem.at[RS], rs_sem, to_across).wait_recv()
@@ -536,7 +536,8 @@
 
 
 def finish(
-    g_in, u_in, mix_in, hid_in, g_out, u_out, mix_out, hid_out, shards, mix32, hid32, sem
+    g_in, u_in, mix_hbm, hid_hbm, g_out, u_out, mix_out, hid_out,
+    shards, mix_in, hid_in, mix32, hid32, sem,
 ):
     halves = [pl.ds(0, FF // 2), pl.ds(FF // 2, FF // 2)]
     load, store = [], []
@@ -545,8 +546,14 @@
             held = shards.at[i, :, cols]
             load.append(pltpu.make_async_copy(source.at[:, cols], held, sem.at[2 * i + k]))
             store.append(pltpu.make_async_copy(held, dest.at[:, cols], sem.at[4 + 2 * i + k]))
+    load_hid = pltpu.make_async_copy(hid_hbm, hid_in, sem.at[8])
+    load_mix = pltpu.make_async_copy(mix_hbm, mix_in, sem.at[9])
+    load_hid.start()
+    load_mix.start()
     for copy in load:
         copy.start()
+    load_hid.wait()
+    load_mix.wait()
     lane = lax.broadcasted_iota(jnp.int32, (ROWS, 128), 1)
     for s in range(2):
         mix32[:, s, :] = mix_in[s].astype(F32)
@@ -665,13 +672,15 @@
             jax.ShapeDtypeStruct((ROWS, 2, 512), BF16),
             jax.ShapeDtypeStruct((ROWS, 2, 1792), BF16),
         ),
-        in_specs=[anywhere, anywhere, inside, inside],
+        in_specs=[anywhere] * 4,
         out_specs=(anywhere, anywhere, inside, inside),
         scratch_shapes=[
             vmem((2, 16, FF), BF16),
+            vmem((2, ROWS, 512), BF16),
+            vmem((2, 2, 4, ROWS, 256), BF16),
             vmem((ROWS, 2, 512), F32),
             vmem((ROWS, 2, 1792), F32),
-            dma((8,)),
+            dma((10,)),
         ],
         compiler_params=pltpu.CompilerParams(vmem_limit_bytes=56 * 1024 * 1024),
     )(gate_updated, up_updated, mixed, hidden)

time: 75 us -> 74 us (0.987)
  Pallas kernels: 74.2 us -> 73.3 us
    pallas_call x1, Pallas kernels: 3.74 us -> 2.88 us  [on_device(): pl.pallas_call(finish, out_shape=(shard, shard, jax.ShapeDtypeStruct((ROW...]
where the time goes in v4:
time: 74 us; the launch traced here: 73.9 us
  Pallas kernels  73.3 us (99%)
    pallas_call x1, Pallas kernels, on_device(): pl.pallas_call(kernel, out_shape=(shard, shard, jax.ShapeDtypeStruct((2,...  70.4 us
    pallas_call x1, Pallas kernels, on_device(): pl.pallas_call(finish, out_shape=(shard, shard, jax.ShapeDtypeStruct((ROW...  2.88 us

profile of v4, /device:TPU:1, one launch (start us, length us, event | category | flops | bytes accessed | tf_op | source)
XLA Modules:
  0.0 73.9 jit_solution(3508040307560026673)
XLA Ops:
  0.6 70.4 %shard_map.192 = (bf16[16,14336]{1,0:T(8,128)(2,1)}, bf16[16,14336]{1,0:T(8,128)(2,1)}, bf16[2,32,512]{2,1,0:T(8,128)(2,1)}, bf16[2,2,4,32,256]{4,3,2,1,0:T(8,128)(2,1)}) custom-call(s32[32]{0:T(128)} %len_in.1, bf16[16,14336]{1,0:T(8,128)(2,1)} %gp.1, bf16[16,14336]{1,0:T(8,128)(2,1)} %up.1, bf16[16,14336]{1,0:T(8,128)(2,1)} %gg.1, bf16[16,14336]{1,0:T(8,128)(2,1)} %ug.1, ...), custom_call_target="tpu_custom_call" | custom-call | tf_op jit(solution)/shard_map/pallas_call | solution.py:606
  71.0 2.9 %shard_map.193 = (bf16[16,14336]{1,0:T(8,128)(2,1)}, bf16[16,14336]{1,0:T(8,128)(2,1)}, bf16[32,2,512]{2,1,0:T(2,128)(2,1)}, bf16[32,2,1792]{2,1,0:T(2,128)(2,1)}) custom-call(bf16[16,14336]{1,0:T(8,128)(2,1)} %get-tuple-element.8.g_in, bf16[16,14336]{1,0:T(8,128)(2,1)} %get-tuple-element.9.u_in, bf16[2,32,512]{2,1,0:T(8,128)(2,1)} %get-tuple-element.10.mix_hbm, ...), custom_call_target="tpu_custom_call" | custom-call | tf_op jit(solution)/shard_map/pallas_call | solution.py:667

commit v5 on v4

--- a/solution.py
+++ b/solution.py
@@ -176,24 +176,19 @@
             place(x, dest // NZ, dest % NZ, c),
         ).start()
 
-    def first_chunks(dest):
-        gate, upper = updated((dest // 2) * PAIR + (dest % 2) * 512, 256)
-        fill(sbuf0.at[dest], (gate[0], upper[0]))
-        fill(sbuf1.at[dest], (gate[1], upper[1]))
-
-    @pl.loop(1, PLANE)
-    def _(t):
-        dest = (position + t) % PLANE
-        first_chunks(dest)
-        send_block(0, dest)
-
-    @pl.loop(1, PLANE)
-    def _(t):
-        send_block(1, (position + t) % PLANE)
-
-    first_chunks(position)
-    wbuf0[x_lo, z, c, y, h] = sbuf0[position]
-    wbuf1[x_lo, z, c, y, h] = sbuf1[position]
+    def early_chunk(q, dest):
+        gate, upper = updated((dest // 2) * PAIR + (dest % 2) * 512 + q * 128, 128)
+        fill(sbufs[q].at[dest], (gate[0], upper[0]))
+
+    for q in range(2):
+        @pl.loop(1, PLANE)
+        def _(t, q=q):
+            dest = (position + t) % PLANE
+            early_chunk(q, dest)
+            send_block(q, dest)
+
+        early_chunk(q, position)
+        wbufs[q][x_lo, z, c, y, h] = sbufs[q][position]
 
     def last_chunk(pair):
         gate, upper = updated(pair * PAIR + 256, 256)

time: 74 us -> 74.2 us (level)
  no operation moved by 1% of the time
where the time goes in v5:
time: 74.2 us; the launch traced here: 74.1 us
  Pallas kernels  73.4 us (99%)
    pallas_call x1, Pallas kernels, on_device(): pl.pallas_call(kernel, out_shape=(shard, shard, jax.ShapeDtypeStruct((2,...  70.6 us
    pallas_call x1, Pallas kernels, on_device(): pl.pallas_call(finish, out_shape=(shard, shard, jax.ShapeDtypeStruct((ROW...  2.88 us

profile of v5, /device:TPU:1, one launch (start us, length us, event | category | flops | bytes accessed | tf_op | source)
XLA Modules:
  0.0 74.1 jit_solution(10021499026933990667)
XLA Ops:
  0.6 70.6 %shard_map.192 = (bf16[16,14336]{1,0:T(8,128)(2,1)}, bf16[16,14336]{1,0:T(8,128)(2,1)}, bf16[2,32,512]{2,1,0:T(8,128)(2,1)}, bf16[2,2,4,32,256]{4,3,2,1,0:T(8,128)(2,1)}) custom-call(s32[32]{0:T(128)} %len_in.1, bf16[16,14336]{1,0:T(8,128)(2,1)} %gp.1, bf16[16,14336]{1,0:T(8,128)(2,1)} %up.1, bf16[16,14336]{1,0:T(8,128)(2,1)} %gg.1, bf16[16,14336]{1,0:T(8,128)(2,1)} %ug.1, ...), custom_call_target="tpu_custom_call" | custom-call | tf_op jit(solution)/shard_map/pallas_call | solution.py:601
  71.2 2.9 %shard_map.193 = (bf16[16,14336]{1,0:T(8,128)(2,1)}, bf16[16,14336]{1,0:T(8,128)(2,1)}, bf16[32,2,512]{2,1,0:T(2,128)(2,1)}, bf16[32,2,1792]{2,1,0:T(2,128)(2,1)}) custom-call(bf16[16,14336]{1,0:T(8,128)(2,1)} %get-tuple-element.8.g_in, bf16[16,14336]{1,0:T(8,128)(2,1)} %get-tuple-element.9.u_in, bf16[2,32,512]{2,1,0:T(8,128)(2,1)} %get-tuple-element.10.mix_hbm, ...), custom_call_target="tpu_custom_call" | custom-call | tf_op jit(solution)/shard_map/pallas_call | solution.py:662
